TPU v7x, 32 devices: a whole 2x2x4 slice. The times are simulated.
32 devices in a mesh: groups: 2 (over x), row: 4 (over y, core), col: 4 (over z).
Axes of the slice: x: 2, y: 2, z: 4, core: 2. Of those that a mesh axis runs over, the one named last changes fastest.
Arguments:
- positions: float32 [3, 32768], P(None, ('groups', 'row', 'col')), parts along dimension 1, may hold values from -6 to 6
- strengths: float32 [3, 32768], P(None, ('groups', 'row', 'col')), parts along dimension 1, may hold values from -6 to 6
- cores: float32 [32768], P(('groups', 'row', 'col')), parts along dimension 0, may hold values from 0.3 to 1
- order: int32 [32768], P(('groups', 'row', 'col')), parts along dimension 0, may hold values from 0 to 1023, as said below
- tile_counts: int32 [256], P(('groups', 'row', 'col')), parts along dimension 0, may hold values from 32 to 128
- pair_slots: int32 [2, 2048], P(None, ('groups', 'row', 'col')), parts along dimension 1, may hold values from 0 to 31, as said below
- pair_count: int32 [32], P(('groups', 'row', 'col')), parts along dimension 0, may hold values from 16 to 64, as said below
Outputs:
- velocity: float32 [3, 32768], P(None, ('groups', 'row', 'col')), parts along dimension 1
- stretching: float32 [3, 32768], P(None, ('groups', 'row', 'col')), parts along dimension 1
There are 2 independent parts, one for each index of `groups`. A program takes and returns all parts, laid end to end along the dimension named above; each array names one. Nothing has to cross between parts.
Inputs may be any that keep to these rules, and one draw needn't show every extreme that they name: `order`: each device's block of 1024 entries is a permutation of 0 to 1023. `pair_slots`: row 0 is below 32, row 1 below 32; the first 8 slots of every device pair each of its own tiles with itself. `pair_count`: some device has all its slots live.
All inputs are finite; a program needn't handle non-finite values.
Results may differ from a plain program's by a relative error of at most 0.0001.
Values sent between devices are 32-bit elements; how exact they have to be, the bound alone decides.
A program may use at most 64 MiB of HBM per device.

v0:
```python
import math

import jax
import jax.numpy as jnp
from jax import lax
from jax.sharding import PartitionSpec as P

TILE = 128
PAIR_BLOCK = 8


biot_factor = -1.0 / (4.0 * math.pi)


def cross_product(left, right):
    return jnp.stack(
        [
            left[1] * right[2] - left[2] * right[1],
            left[2] * right[0] - left[0] * right[2],
            left[0] * right[1] - left[1] * right[0],
        ]
    )


def pair_terms(target, source, weight_t, weight_r):
    target_pos = target[0:3, :, :, None]
    source_pos = source[0:3, :, None, :]
    target_str = target[3:6, :, :, None]
    source_str = source[3:6, :, None, :]
    offset = target_pos - source_pos
    sigma_sq = 0.5 * (target[6][:, :, None] ** 2 + source[6][:, None, :] ** 2)
    rho_sq = (offset[0] * offset[0] + offset[1] * offset[1] + offset[2] * offset[2]) / sigma_sq
    inverse = lax.rsqrt(rho_sq + 1.0)
    inverse_sq = inverse * inverse
    inverse_five = inverse_sq * inverse_sq * inverse
    core_cube = sigma_sq * jnp.sqrt(sigma_sq)
    smooth = (rho_sq + 2.5) * inverse_five / core_cube
    gradient = -3.0 * (rho_sq + 3.5) * inverse_five * inverse_sq / (core_cube * sigma_sq)
    cross_src = cross_product(offset, source_str)
    cross_tgt = cross_product(offset, target_str)
    along_tgt = jnp.sum(target_str * offset, axis=0)
    along_src = jnp.sum(source_str * offset, axis=0)
    smooth_t = smooth * weight_t[:, None, None]
    grad_t = gradient * weight_t[:, None, None]
    vel_target = biot_factor * jnp.sum(smooth_t * cross_src, axis=-1)
    mix_target = jnp.sum(smooth_t * source_str, axis=-1)
    str_target = biot_factor * (
        cross_product(target[3:6], mix_target) + jnp.sum(grad_t * along_tgt * cross_src, axis=-1)
    )
    smooth_r = smooth * weight_r[:, None, None]
    grad_r = gradient * weight_r[:, None, None]
    vel_source = -biot_factor * jnp.sum(smooth_r * cross_tgt, axis=-2)
    mix_source = jnp.sum(smooth_r * target_str, axis=-2)
    str_source = biot_factor * (
        -cross_product(mix_source, source[3:6]) + jnp.sum(grad_r * along_src * cross_tgt, axis=-2)
    )
    return (
        jnp.concatenate([vel_target, str_target], axis=0),
        jnp.concatenate([vel_source, str_source], axis=0),
    )


def shards(positions, strengths, cores, order, tile_counts, pair_slots, pair_count):
    tiles_here = tile_counts.shape[0]
    per_dev = tiles_here * TILE
    nrows = lax.axis_size("row")
    ncols = lax.axis_size("col")
    row_index = lax.axis_index("row")
    col_index = lax.axis_index("col")
    lanes = jnp.arange(per_dev, dtype=jnp.int32) % TILE
    live = (lanes < jnp.repeat(tile_counts, TILE)).astype(jnp.float32)
    packed = jnp.concatenate(
        [positions[:, order], strengths[:, order] * live, cores[order][None, :]], axis=0
    )
    gathered = lax.all_gather(packed, ("row", "col"), axis=1, tiled=True)
    layered = gathered.reshape(7, nrows, ncols, per_dev)
    row_block = lax.dynamic_index_in_dim(layered, row_index, 1, keepdims=False).reshape(
        7, ncols * tiles_here, TILE
    )
    col_block = lax.dynamic_index_in_dim(layered, col_index, 2, keepdims=False).reshape(
        7, nrows * tiles_here, TILE
    )
    num_slots = pair_slots.shape[1]
    count = pair_count[0]
    first = pair_slots[0]
    second = pair_slots[1]
    target_tile = row_index * (ncols * tiles_here) + first
    source_tile = (second // tiles_here * ncols + col_index) * tiles_here + second % tiles_here
    alive = (jnp.arange(num_slots, dtype=jnp.int32) < count).astype(jnp.float32)
    react = alive * (target_tile != source_tile).astype(jnp.float32)

    def visit(block_index, sums):
        target_sum, source_sum = sums
        start = block_index * PAIR_BLOCK
        tgt_idx = lax.dynamic_slice_in_dim(first, start, PAIR_BLOCK)
        src_idx = lax.dynamic_slice_in_dim(second, start, PAIR_BLOCK)
        weight_t = lax.dynamic_slice_in_dim(alive, start, PAIR_BLOCK)
        weight_r = lax.dynamic_slice_in_dim(react, start, PAIR_BLOCK)
        tgt_terms, src_terms = pair_terms(
            row_block[:, tgt_idx], col_block[:, src_idx], weight_t, weight_r
        )
        return (target_sum.at[:, tgt_idx].add(tgt_terms), source_sum.at[:, src_idx].add(src_terms))

    start_sums = (
        jnp.zeros((6, ncols * tiles_here, TILE), jnp.float32),
        jnp.zeros((6, nrows * tiles_here, TILE), jnp.float32),
    )
    target_sum, source_sum = lax.fori_loop(0, num_slots // PAIR_BLOCK, visit, start_sums)
    whole = jnp.zeros((6, nrows, ncols, per_dev), jnp.float32)
    whole = whole.at[:, row_index].add(target_sum.reshape(6, ncols, per_dev))
    whole = whole.at[:, :, col_index].add(source_sum.reshape(6, nrows, per_dev))
    total = lax.psum_scatter(
        whole.reshape(6, nrows * ncols * per_dev), ("row", "col"), scatter_dimension=1, tiled=True
    )
    total = total * live
    return (total[0:3], total[3:6])


def solution(mesh):
    in_specs = (
        P(None, ("groups", "row", "col")),
        P(None, ("groups", "row", "col")),
        P(("groups", "row", "col")),
        P(("groups", "row", "col")),
        P(("groups", "row", "col")),
        P(None, ("groups", "row", "col")),
        P(("groups", "row", "col")),
    )
    out_specs = (P(None, ("groups", "row", "col")), P(None, ("groups", "row", "col")))
    return jax.shard_map(shards, mesh=mesh, in_specs=in_specs, out_specs=out_specs, check_vma=False)
```

profile of v0, /device:TPU:0, one launch (start us, length us, event | category | flops | bytes accessed | tf_op | source)
XLA Modules:
  0.0 189.9 jit_solution(1324412315993158245)
XLA Ops:
  7.2 0.7 fusion.13
  7.9 0.9 copy.87
  8.9 0.7 fusion.17
  9.6 2.8 %gather_fusion.3 = f32[1024,3]{1,0:T(8,128)S(1)} fusion(f32[3,1024]{0,1:T(8,128)S(1)} %copy.87, s32[1024]{0:T(1024)S(1)} %fusion.13), kind=kCustom, calls=%fused_computation.3 | custom fusion | bytes 28672 | tf_op jit(solution)/shard_map/gather | solution.py:73
  13.1 2.8 %gather_fusion.2 = f32[1024,3]{1,0:T(8,128)S(1)} fusion(f32[3,1024]{0,1:T(8,128)S(1)} %copy.86, s32[1024]{0:T(1024)S(1)} %fusion.13), kind=kCustom, calls=%fused_computation.2 | custom fusion | bytes 28672 | tf_op jit(solution)/shard_map/gather | solution.py:73
  16.1 4.5 %gather_fusion.4 = f32[1024]{0:T(1024)S(1)} fusion(f32[1024]{0:T(1024)S(1)} %copy-done, s32[1024]{0:T(1024)S(1)} %fusion.13), kind=kCustom, calls=%fused_computation.4 | custom fusion | bytes 12288 | tf_op jit(solution)/shard_map/gather | solution.py:73
  20.7 38.7 %all_gather.3 = f32[7,16384]{1,0:T(8,128)S(1)} all-gather(f32[7,1024]{1,0:T(8,128)S(1)} %pad_maximum_fusion.2), channel_id=1, replica_groups=mesh['groups'=2,'row'=4,'col'=4] {'row','col'}, dimensions={1}, use_global_device_ids=true | all-gather | bytes 487424 | tf_op jit(solution)/shard_map/all_gather | solution.py:75
  60.8 62.2 %while.17 = (s32[]{:T(128)}, f32[6,32,128]{2,0,1:T(8,128)S(1)}, f32[6,32,128]{2,0,1:T(8,128)S(1)}, s32[64]{0:T(128)S(1)}, f32[7,32,128]{2,0,1:T(8,128)S(1)}, /*i...) while((s32[]{:T(128)}, f32[6,32,128]{2,0,1:T(8,128)S(1)}, ...), condition=%wide.region_12.13_spmd, body=%wide.region_1.12_spmd.sunk | while | flops 15791158 | bytes 19481304 | solution.py:108
  62.1 0.9 multiply_reduce_fusion.11
  64.9 0.6 multiply_reduce_fusion.13
  65.6 0.8 scatter_fusion.1
  66.4 1.3 multiply_reduce_fusion.12
  67.8 0.8 scatter_fusion
  69.9 0.9 multiply_reduce_fusion.11
  72.7 0.6 multiply_reduce_fusion.13
  73.4 0.8 scatter_fusion.1
  74.2 1.3 multiply_reduce_fusion.12
  75.6 0.8 scatter_fusion
  77.6 0.9 multiply_reduce_fusion.11
  81.2 0.8 scatter_fusion.1
  82.0 1.3 multiply_reduce_fusion.12
  83.3 0.8 scatter_fusion
  85.4 0.9 multiply_reduce_fusion.11
  89.0 0.8 scatter_fusion.1
  89.7 1.3 multiply_reduce_fusion.12
  91.1 0.8 scatter_fusion
  93.2 0.9 multiply_reduce_fusion.11
  96.7 0.8 scatter_fusion.1
  97.5 1.3 multiply_reduce_fusion.12
  98.9 0.8 scatter_fusion
  101.0 0.9 multiply_reduce_fusion.11
  104.5 0.8 scatter_fusion.1
  105.3 1.3 multiply_reduce_fusion.12
  106.6 0.8 scatter_fusion
  108.7 0.9 multiply_reduce_fusion.11
  112.3 0.8 scatter_fusion.1
  113.0 1.3 multiply_reduce_fusion.12
  114.4 0.8 scatter_fusion
  116.5 0.9 multiply_reduce_fusion.11
  120.0 0.8 scatter_fusion.1
  120.8 1.3 multiply_reduce_fusion.12
  122.2 0.8 scatter_fusion
  123.0 0.7 and_reduce_fusion
  124.6 0.7 scatter-add.32
  125.4 0.7 fusion.11
  126.3 1.1 reshape.199
  127.4 54.3 %reduce-scatter.2.cloned.1.call-done = f32[6,1024]{1,0:T(8,128)} async-done(((f32[6,16384]{1,0:T(8,128)}), f32[6,1024]{1,0:T(8,128)}) %reduce-scatter.2.cloned.1.call-update) | async-done | bytes 24592 | tf_op jit(solution)/shard_map/reduce_scatter | solution.py:112
  181.7 0.8 broadcast_multiply_fusion.2
  (251 shorter events, 32.7 us)
Async XLA Ops:
  7.2 8.9 %copy-start = (f32[1024]{0:T(1024)S(1)}, f32[1024]{0:T(1024)}, u32[]{:S(2)}) copy-start(f32[1024]{0:T(1024)} %param.15) | copy-start | bytes 12292
  7.2 5.6 %copy-start.1 = (f32[3,1024]{1,0:T(4,128)S(1)}, f32[3,1024]{1,0:T(4,128)}, u32[]{:S(2)}) copy-start(f32[3,1024]{1,0:T(4,128)} %param.13) | copy-start | bytes 36868
  7.2 174.5 %reduce-scatter.2.cloned.1.call-start = ((), (), s32[]{:S(2)}) async-start(), calls=%async_computation.1 | async-start | bytes 557056 | tf_op jit(solution)/shard_map/reduce_scatter | solution.py:112
  20.6 40.1 %copy-start.2 = (s32[2,64]{1,0:T(2,128)S(1)}, s32[2,64]{1,0:T(2,128)}, u32[]{:S(2)}) copy-start(s32[2,64]{1,0:T(2,128)} %param.18) | copy-start | bytes 1540
  60.8 62.2 %copy-start.3 = (s32[4]{0:T(128)S(1)}, s32[4]{0:T(128)}, u32[]{:S(2)}) copy-start(s32[4]{0:T(128)} %constant.186.clone.1) | copy-start | bytes 52
  60.8 62.2 %copy-start.4 = (s32[4]{0:T(128)S(1)}, s32[4]{0:T(128)}, u32[]{:S(2)}) copy-start(s32[4]{0:T(128)} %constant.197.clone.1) | copy-start | bytes 52
Sparse Core Ops, SparseCore 0:
  127.5 54.1 reduce-scatter.1
where the time goes:
time: 190 us
  other arithmetic  54.3 us (29%)
  waiting for transfers between devices  54.3 us (29%)
  blocking collectives  38.7 us (20%)
  local copies, waits for them, and re-layouts  25.9 us (14%)
  between operations  15 us (8%)
    reduce_scatter x1, waiting for transfers between devices, shards(): lax.psum_scatter(whole.reshape(6, nrows * ncols * per_dev), ('row', 'col'...  54.3 us
    all_gather x1, blocking collectives, shards(): gathered = lax.all_gather(packed, ('row', 'col'), axis=1, tiled=True)  38.7 us
    reduce_sum x8, other arithmetic, pair_terms(): vel_target = biot_factor * jnp.sum(smooth_t * cross_src, axis=-1)  10.3 us
    reduce_sum x8, other arithmetic, pair_terms(): along_src = jnp.sum(source_str * offset, axis=0)  7.02 us
    scatter-add x8, other arithmetic, visit(): source_sum.at[:, src_idx].add(src_terms)  6.22 us
    scatter-add x8, other arithmetic, visit(): target_sum.at[:, tgt_idx].add(tgt_terms)  6.22 us
    reduce_sum x8, other arithmetic, pair_terms(): vel_source = -biot_factor * jnp.sum(smooth_r * cross_tgt, axis=-2)  5.09 us
    mul x8, other arithmetic, pair_terms(): grad_t * along_tgt * cross_src  4.97 us
  transfers between devices with their start and end apart: 1, of which 1 were waited for; matrix products, arithmetic and copies ran while one was open for 0% of the time, Pallas kernels for 0%

commit v1 on v0

v1 whole, which is shorter than its diff:
```python
import functools
import math

import jax
import jax.numpy as jnp
from jax import lax
from jax.experimental import pallas as pl
from jax.experimental.pallas import tpu as pltpu
from jax.sharding import PartitionSpec as P

TILE = 128
MESH = pl.DeviceIdType.MESH
VMEM = pl.BlockSpec(memory_space=pltpu.VMEM)
SMEM = pl.BlockSpec(memory_space=pltpu.SMEM)
UNROLL = 2
CHUNK = 16

biot_factor = -1.0 / (4.0 * math.pi)


def peers(nrows, ncols):
    return [("col", k) for k in range(1, ncols)] + [("row", k) for k in range(1, nrows)]


def greet(nrows, ncols):
    barrier = pltpu.get_barrier_semaphore()
    for axis, k in peers(nrows, ncols):
        size = ncols if axis == "col" else nrows
        other = lax.rem(lax.axis_index(axis) + k, size)
        pl.semaphore_signal(barrier, inc=1, device_id={axis: other}, device_id_type=MESH)
    return barrier


def gather_kernel(nrows, ncols, tiles, pos, strg, cores, order, counts, row_out, col_out, raw, mine, send, recv):
    barrier = greet(nrows, ncols)
    row = lax.axis_index("row")
    col = lax.axis_index("col")
    lane = lax.broadcasted_iota(jnp.int32, (8, TILE), 1)
    sub = lax.broadcasted_iota(jnp.int32, (8, TILE), 0)
    for t in range(tiles):
        part = slice(t * TILE, (t + 1) * TILE)
        raw[t] = jnp.zeros((8, TILE), jnp.float32)
        raw[t, 0:3, :] = pos[:, part]
        raw[t, 3:6, :] = strg[:, part]
        raw[t, 6:7, :] = cores[t : t + 1, :]
    for t in range(tiles):
        spot = jnp.broadcast_to(order[t : t + 1, :], (8, TILE))
        inner = spot % TILE
        outer = spot // TILE
        found = jnp.zeros((8, TILE), jnp.float32)
        for s in range(tiles):
            found = jnp.where(outer == s, jnp.take_along_axis(raw[s], inner, axis=1), found)
        keep = (lane < counts[t]) | (sub < 3) | (sub > 5)
        mine[t] = jnp.where(keep, found, 0.0)
    pl.semaphore_wait(barrier, nrows + ncols - 2)
    copies = []
    for n, (axis, k) in enumerate(peers(nrows, ncols)):
        size, me = (ncols, col) if axis == "col" else (nrows, row)
        dest = row_out if axis == "col" else col_out
        copy = pltpu.make_async_remote_copy(
            src_ref=mine,
            dst_ref=dest.at[me],
            send_sem=send.at[n],
            recv_sem=recv.at[n],
            device_id={axis: lax.rem(me + k, size)},
            device_id_type=MESH,
        )
        copy.start()
        copies.append(copy)
    row_out[col] = mine[...]
    col_out[row] = mine[...]
    for copy in copies:
        copy.wait()


def split(value):
    high = value.astype(jnp.bfloat16)
    return high, (value - high.astype(jnp.float32)).astype(jnp.bfloat16)


def pair_kernel(nrows, ncols, tiles, slots, count, row_blk, col_blk, row_out, col_out,
                across, row_w, col_w, row_acc, col_acc, tgt_buf, src_buf):
    row = lax.axis_index("row")
    col = lax.axis_index("col")
    row_acc[...] = jnp.zeros_like(row_acc)
    col_acc[...] = jnp.zeros_like(col_acc)

    def features(block):
        x = block[0:3]
        a = block[3:6]
        b = [x[1] * a[2] - x[2] * a[1], x[2] * a[0] - x[0] * a[2], x[0] * a[1] - x[1] * a[0]]
        vectors = jnp.concatenate([a] + [v[None, :] for v in b], axis=0)
        high = vectors.astype(jnp.bfloat16).astype(jnp.float32)
        zeros = jnp.zeros((4, TILE), jnp.float32)
        both = jnp.concatenate([high, vectors - high, zeros], axis=0).astype(jnp.bfloat16)
        return jnp.concatenate([both, both], axis=1)

    def prepare_row(t, _):
        block = row_blk[t]
        across[t] = block.T
        row_w[t] = features(block)
        return 0

    def prepare_col(t, _):
        col_w[t] = features(col_blk[t])
        return 0

    lax.fori_loop(0, row_blk.shape[0], prepare_row, 0)
    lax.fori_loop(0, col_blk.shape[0], prepare_col, 0)

    def visit(step, _):
        for u in range(UNROLL):
            s = step * UNROLL + u
            ti = slots[0, s]
            sj = slots[1, s]
            alive = jnp.where(s < count[0], 1.0, 0.0)
            gi = row * (ncols * tiles) + ti
            gj = ((sj // tiles) * ncols + col) * tiles + sj % tiles
            react = jnp.where(gi != gj, alive, 0.0)
            src = col_blk[sj]
            xj = [src[k : k + 1, :] for k in range(7)]
            hj = 0.5 * xj[6] * xj[6]
            for c in range(TILE // CHUNK):
                at = slice(c * CHUNK, (c + 1) * CHUNK)
                at2 = slice(TILE + c * CHUNK, TILE + (c + 1) * CHUNK)
                tgt = across[ti, at, :]
                xi = [tgt[:, k : k + 1] for k in range(7)]
                hi = 0.5 * xi[6] * xi[6]
                dx = xi[0] - xj[0]
                dy = xi[1] - xj[1]
                dz = xi[2] - xj[2]
                s2 = hi + hj
                d = dx * dx + dy * dy + dz * dz + s2
                inv = lax.rsqrt(d)
                inv2 = inv * inv
                inv3 = inv2 * inv
                w = s2 * (inv3 * inv2)
                q = inv3 + 1.5 * w
                f = (q + w) * inv2
                g = f * (xi[3] * dx + xi[4] * dy + xi[5] * dz)
                h = f * (xj[3] * dx + xj[4] * dy + xj[5] * dz)
                q1, q2 = split(q)
                g1, g2 = split(g)
                h1, h2 = split(h)
                tgt_buf[u, at, 0:TILE] = q1
                tgt_buf[u, at, TILE:] = q2
                tgt_buf[u, at2, 0:TILE] = g1
                tgt_buf[u, at2, TILE:] = g2
                src_buf[u, at, 0:TILE] = q1
                src_buf[u, at, TILE:] = h1
                src_buf[u, at2, 0:TILE] = q2
                src_buf[u, at2, TILE:] = h2
            out_t = lax.dot_general(col_w[sj], tgt_buf[u], (((1,), (1,)), ((), ())),
                                    preferred_element_type=jnp.float32)
            out_s = lax.dot_general(row_w[ti], src_buf[u], (((1,), (0,)), ((), ())),
                                    preferred_element_type=jnp.float32)
            row_acc[ti] += alive * out_t
            col_acc[sj] += react * out_s
        return 0

    lax.fori_loop(0, (count[0] + (UNROLL - 1)) // UNROLL, visit, 0)

    def finish(block, acc, out, sign):
        x = [block[:, k, :] for k in range(3)]
        a = [block[:, 3 + k, :] for k in range(3)]
        qs = [acc[:, k, 0:TILE] + acc[:, 6 + k, 0:TILE] for k in range(6)]
        fs = [acc[:, k, TILE:] + acc[:, 6 + k, TILE:] for k in range(6)]
        for k in range(3):
            m, n = (k + 1) % 3, (k + 2) % 3
            velocity = x[m] * qs[n] - x[n] * qs[m] - qs[3 + k]
            steep = x[m] * fs[n] - x[n] * fs[m] - fs[3 + k]
            turn = a[m] * qs[n] - a[n] * qs[m]
            out[:, k, :] = biot_factor * velocity
            out[:, 3 + k, :] = biot_factor * (turn - (3.0 * sign) * steep)
            if k < 2:
                out[:, 6 + k, :] = jnp.zeros_like(velocity)

    finish(row_blk, row_acc, row_out, 1.0)
    finish(col_blk, col_acc, col_out, -1.0)


def scatter_kernel(nrows, ncols, tiles, row_terms, col_terms, counts, vel, stretch, held, send, recv):
    barrier = greet(nrows, ncols)
    row = lax.axis_index("row")
    col = lax.axis_index("col")
    pl.semaphore_wait(barrier, nrows + ncols - 2)
    copies = []
    for n, (axis, k) in enumerate(peers(nrows, ncols)):
        size, me = (ncols, col) if axis == "col" else (nrows, row)
        terms = row_terms if axis == "col" else col_terms
        other = lax.rem(me + k, size)
        copy = pltpu.make_async_remote_copy(
            src_ref=terms.at[other],
            dst_ref=held.at[n],
            send_sem=send.at[n],
            recv_sem=recv.at[n],
            device_id={axis: other},
            device_id_type=MESH,
        )
        copy.start()
        copies.append(copy)
    total = row_terms[col] + col_terms[row]
    for n, copy in enumerate(copies):
        copy.wait_recv()
        total = total + held[n]
    lane = lax.broadcasted_iota(jnp.int32, (8, TILE), 1)
    for t in range(tiles):
        part = slice(t * TILE, (t + 1) * TILE)
        value = jnp.where(lane < counts[t], total[t], 0.0)
        vel[:, part] = value[0:3]
        stretch[:, part] = value[3:6]
    for copy in copies:
        copy.wait_send()


def shards(nrows, ncols, positions, strengths, cores, order, tile_counts, pair_slots, pair_count):
    tiles = tile_counts.shape[0]
    others = nrows + ncols - 2
    f32 = jnp.float32
    row_blk, col_blk = pl.pallas_call(
        functools.partial(gather_kernel, nrows, ncols, tiles),
        out_shape=(
            jax.ShapeDtypeStruct((ncols, tiles, 8, TILE), f32),
            jax.ShapeDtypeStruct((nrows, tiles, 8, TILE), f32),
        ),
        in_specs=[VMEM, VMEM, VMEM, VMEM, SMEM],
        out_specs=(VMEM, VMEM),
        scratch_shapes=[
            pltpu.VMEM((tiles, 8, TILE), f32),
            pltpu.VMEM((tiles, 8, TILE), f32),
            pltpu.SemaphoreType.DMA((others,)),
            pltpu.SemaphoreType.DMA((others,)),
        ],
        compiler_params=pltpu.CompilerParams(collective_id=0, has_side_effects=True),
        name="gather_tiles",
    )(positions, strengths, cores.reshape(tiles, TILE), order.reshape(tiles, TILE), tile_counts)
    nt, ns = ncols * tiles, nrows * tiles
    row_terms, col_terms = pl.pallas_call(
        functools.partial(pair_kernel, nrows, ncols, tiles),
        out_shape=(
            jax.ShapeDtypeStruct((nt, 8, TILE), f32),
            jax.ShapeDtypeStruct((ns, 8, TILE), f32),
        ),
        in_specs=[SMEM, SMEM, VMEM, VMEM],
        out_specs=(VMEM, VMEM),
        scratch_shapes=[
            pltpu.VMEM((nt, TILE, 8), f32),
            pltpu.VMEM((nt, 16, 2 * TILE), jnp.bfloat16),
            pltpu.VMEM((ns, 16, 2 * TILE), jnp.bfloat16),
            pltpu.VMEM((nt, 16, 2 * TILE), f32),
            pltpu.VMEM((ns, 16, 2 * TILE), f32),
            pltpu.VMEM((UNROLL, 2 * TILE, 2 * TILE), jnp.bfloat16),
            pltpu.VMEM((UNROLL, 2 * TILE, 2 * TILE), jnp.bfloat16),
        ],
        compiler_params=pltpu.CompilerParams(vmem_limit_bytes=32 * 1024 * 1024),
        name="pair_terms",
    )(pair_slots, pair_count, row_blk.reshape(nt, 8, TILE), col_blk.reshape(ns, 8, TILE))
    return pl.pallas_call(
        functools.partial(scatter_kernel, nrows, ncols, tiles),
        out_shape=(
            jax.ShapeDtypeStruct((3, tiles * TILE), f32),
            jax.ShapeDtypeStruct((3, tiles * TILE), f32),
        ),
        in_specs=[VMEM, VMEM, SMEM],
        out_specs=(VMEM, VMEM),
        scratch_shapes=[
            pltpu.VMEM((others, tiles, 8, TILE), f32),
            pltpu.SemaphoreType.DMA((others,)),
            pltpu.SemaphoreType.DMA((others,)),
        ],
        compiler_params=pltpu.CompilerParams(collective_id=1, has_side_effects=True),
        name="sum_terms",
    )(row_terms.reshape(ncols, tiles, 8, TILE), col_terms.reshape(nrows, tiles, 8, TILE), tile_counts)


def solution(mesh):
    whole = ("groups", "row", "col")
    in_specs = (P(None, whole), P(None, whole), P(whole), P(whole), P(whole), P(None, whole), P(whole))
    out_specs = (P(None, whole), P(None, whole))
    body = functools.partial(shards, mesh.shape["row"], mesh.shape["col"])
    return jax.shard_map(body, mesh=mesh, in_specs=in_specs, out_specs=out_specs, check_vma=False)
```

time: 190 us -> 48.9 us (0.26)
  other arithmetic: 54.3 us -> 0 us
  waiting for transfers between devices: 54.3 us -> 0 us
  Pallas kernels: 0 us -> 42 us
  blocking collectives: 38.7 us -> 0 us
  local copies, waits for them, and re-layouts: 25.9 us -> 5.72 us
  between operations: 15 us -> 1.33 us
    reduce_scatter x1 -> x0, waiting for transfers between devices: 54.3 us -> none  [shards(): lax.psum_scatter(whole.reshape(6, nrows * ncols * per_dev), ('row', 'col'...]
    pallas_call x0 -> x3, Pallas kernels: none -> 42 us  [the longest x1 21.4 us: shards(): pl.pallas_call(functools.partial(scatter_kernel, nrows, ncols, tiles), ou...]
    all_gather x1 -> x0, blocking collectives: 38.7 us -> none  [shards(): gathered = lax.all_gather(packed, ('row', 'col'), axis=1, tiled=True)]
    reduce_sum x24 -> x0, other arithmetic: 22.4 us -> none  [the longest x8 10.3 us: pair_terms(): vel_target = biot_factor * jnp.sum(smooth_t * cross_src, axis=-1)]
    gather x36 -> x0, local copies, waits for them, and re-layouts: 19.4 us -> none  [the longest x1 4.53 us: shards(): cores[order][None, :]]
    scatter-add x17 -> x0, other arithmetic: 13.1 us -> none  [the longest x8 6.22 us: visit(): source_sum.at[:, src_idx].add(src_terms)]
    mul x59 -> x0, other arithmetic: 11 us -> none  [the longest x8 4.97 us: pair_terms(): grad_t * along_tgt * cross_src]
    unnamed x13 -> x14, local copies, waits for them, and re-layouts: 1.21 us -> 5.72 us
  transfers between devices with their start and end apart: 1 -> 0, of which waited for: 1 -> 0; matrix products, arithmetic and copies ran while one was open for 0% -> 0% of each run, Pallas kernels for 0% -> 0%
where the time goes in v1:
time: 48.9 us; the launch traced here: 49 us
  Pallas kernels  42 us (86%)
  local copies, waits for them, and re-layouts  5.72 us (12%)
  between operations  1.33 us (3%)
    pallas_call x1, Pallas kernels, shards(): pl.pallas_call(functools.partial(scatter_kernel, nrows, ncols, tiles), ou...  21.4 us
    pallas_call x1, Pallas kernels, shards(): pl.pallas_call(functools.partial(gather_kernel, nrows, ncols, tiles), out...  10.4 us
    pallas_call x1, Pallas kernels, shards(): pl.pallas_call(functools.partial(pair_kernel, nrows, ncols, tiles), out_s...  10.1 us
    unnamed x14, local copies, waits for them, and re-layouts  5.72 us

profile of v1, /device:TPU:0, one launch (start us, length us, event | category | flops | bytes accessed | tf_op | source)
XLA Modules:
  0.0 49.0 jit_solution(9829719295751858658)
XLA Ops:
  1.3 10.4 %gather_tiles.1 = (f32[4,8,8,128]{3,2,1,0:T(8,128)}, f32[4,8,8,128]{3,2,1,0:T(8,128)}) custom-call(f32[3,1024]{1,0:T(4,128)} %pos.1, f32[3,1024]{1,0:T(4,128)} %strg.1, f32[8,128]{1,0:T(8,128)} %bitcast.10, s32[8,128]{1,0:T(8,128)} %bitcast.11, s32[8]{0:T(128)} %counts.3), custom_call_target="tpu_custom_call" | custom-call | tf_op jit(solution)/shard_map/gather_tiles/pallas_call | solution.py:220
  11.7 0.0 copy-start.4
  11.7 0.7 %copy-done.4 = s32[2,64]{1,0:T(2,128)S(1)} copy-done((s32[2,64]{1,0:T(2,128)S(1)}, s32[2,64]{1,0:T(2,128)}, u32[]{:S(2)}) %copy-start.4) | copy-done | bytes 536
  12.4 0.0 copy-start.2
  12.4 0.9 %copy-done.2 = f32[4,8,8,128]{3,2,1,0:T(8,128)S(1)} copy-done((f32[4,8,8,128]{3,2,1,0:T(8,128)S(1)}, f32[4,8,8,128]{3,2,1,0:T(8,128)}, u32[]{:S(2)}) %copy-start.2) | copy-done | bytes 131096
  13.3 0.0 copy-start.3
  13.3 0.9 %copy-done.3 = f32[4,8,8,128]{3,2,1,0:T(8,128)S(1)} copy-done((f32[4,8,8,128]{3,2,1,0:T(8,128)S(1)}, f32[4,8,8,128]{3,2,1,0:T(8,128)}, u32[]{:S(2)}) %copy-start.3) | copy-done | bytes 131096
  14.2 10.1 %pair_terms.1 = (f32[32,8,128]{2,1,0:T(8,128)S(1)}, f32[32,8,128]{2,1,0:T(8,128)S(1)}) custom-call(s32[2,64]{1,0:T(2,128)S(1)} %copy-done.4, s32[1]{0:T(128)S(6)} %copy.11.count, f32[32,8,128]{2,1,0:T(8,128)S(1)} %bitcast.8, f32[32,8,128]{2,1,0:T(8,128)S(1)} %bitcast.9), custom_call_target="tpu_custom_call" | custom-call | tf_op jit(solution)/shard_map/pair_terms/pallas_call | solution.py:238
  24.4 0.0 copy-start
  24.4 0.6 %copy-done = f32[32,8,128]{2,1,0:T(8,128)} copy-done((f32[32,8,128]{2,1,0:T(8,128)}, f32[32,8,128]{2,1,0:T(8,128)S(1)}, u32[]{:S(2)}) %copy-start) | copy-done | bytes 131096
  25.0 0.0 copy-start.1
  25.0 0.7 %copy-done.1 = f32[32,8,128]{2,1,0:T(8,128)} copy-done((f32[32,8,128]{2,1,0:T(8,128)}, f32[32,8,128]{2,1,0:T(8,128)S(1)}, u32[]{:S(2)}) %copy-start.1) | copy-done | bytes 131096
  25.7 21.4 %sum_terms.1 = (f32[3,1024]{1,0:T(4,128)}, f32[3,1024]{1,0:T(4,128)}) custom-call(f32[4,8,8,128]{3,2,1,0:T(8,128)} %bitcast.6, f32[4,8,8,128]{3,2,1,0:T(8,128)} %bitcast.7, s32[8]{0:T(128)} %counts.3), custom_call_target="tpu_custom_call" | custom-call | tf_op jit(solution)/shard_map/sum_terms/pallas_call | solution.py:258
  47.1 0.0 copy-start.5
  47.1 1.3 %copy.12 = f32[3,1024]{1,0:T(4,128)} copy(f32[3,1024]{1,0:T(4,128)} %get-tuple-element.12) | data formatting | bytes 24576
  48.4 0.0 copy-done.5
  48.4 0.6 %copy.13 = f32[3,1024]{1,0:T(4,128)} copy(f32[3,1024]{1,0:T(4,128)S(1)} %copy-done.5) | data formatting | bytes 24576
Async XLA Ops:
  11.7 0.7 %copy-start.4 = (s32[2,64]{1,0:T(2,128)S(1)}, s32[2,64]{1,0:T(2,128)}, u32[]{:S(2)}) copy-start(s32[2,64]{1,0:T(2,128)} %slots.1) | copy-start | bytes 1540
  12.4 0.9 %copy-start.2 = (f32[4,8,8,128]{3,2,1,0:T(8,128)S(1)}, f32[4,8,8,128]{3,2,1,0:T(8,128)}, u32[]{:S(2)}) copy-start(f32[4,8,8,128]{3,2,1,0:T(8,128)} %get-tuple-element.6) | copy-start | bytes 393220
  13.3 0.9 %copy-start.3 = (f32[4,8,8,128]{3,2,1,0:T(8,128)S(1)}, f32[4,8,8,128]{3,2,1,0:T(8,128)}, u32[]{:S(2)}) copy-start(f32[4,8,8,128]{3,2,1,0:T(8,128)} %get-tuple-element.7) | copy-start | bytes 393220
  24.4 0.7 %copy-start = (f32[32,8,128]{2,1,0:T(8,128)}, f32[32,8,128]{2,1,0:T(8,128)S(1)}, u32[]{:S(2)}) copy-start(f32[32,8,128]{2,1,0:T(8,128)S(1)} %get-tuple-element.8) | copy-start | bytes 393220
  25.0 0.7 %copy-start.1 = (f32[32,8,128]{2,1,0:T(8,128)}, f32[32,8,128]{2,1,0:T(8,128)S(1)}, u32[]{:S(2)}) copy-start(f32[32,8,128]{2,1,0:T(8,128)S(1)} %get-tuple-element.9) | copy-start | bytes 393220
  47.1 1.3 %copy-start.5 = (f32[3,1024]{1,0:T(4,128)S(1)}, f32[3,1024]{1,0:T(4,128)}, u32[]{:S(2)}) copy-start(f32[3,1024]{1,0:T(4,128)} %get-tuple-element.13) | copy-start | bytes 36868

commit v2 on v1

v2 whole, which is shorter than its diff:
```python
import functools
import math

import jax
import jax.numpy as jnp
from jax import lax
from jax.experimental import pallas as pl
from jax.experimental.pallas import tpu as pltpu
from jax.sharding import PartitionSpec as P

TILE = 128
MESH = pl.DeviceIdType.MESH
VMEM = pl.BlockSpec(memory_space=pltpu.VMEM)
SMEM = pl.BlockSpec(memory_space=pltpu.SMEM)
UNROLL = 4
CHUNK = 16

biot_factor = -1.0 / (4.0 * math.pi)


def peers(nrows, ncols):
    return [("col", k) for k in range(1, ncols)] + [("row", k) for k in range(1, nrows)]


def greet(nrows, ncols):
    barrier = pltpu.get_barrier_semaphore()
    for axis, k in peers(nrows, ncols):
        size = ncols if axis == "col" else nrows
        other = lax.rem(lax.axis_index(axis) + k, size)
        pl.semaphore_signal(barrier, inc=1, device_id={axis: other}, device_id_type=MESH)
    return barrier


def split(value):
    high = value.astype(jnp.bfloat16)
    return high, (value - high.astype(jnp.float32)).astype(jnp.bfloat16)


def cross(left, right):
    return [left[(k + 1) % 3] * right[(k + 2) % 3] - left[(k + 2) % 3] * right[(k + 1) % 3] for k in range(3)]


def wake_kernel(nrows, ncols, tiles, slots, count, counts, slot_rows, pos, strg, cores, order,
                vel, stretch, raw, row_blk, col_blk, across, stage, row_w, col_w, tgt_buf, src_buf,
                tgt_terms, src_terms, row_sum, col_sum, row_held, col_held, send, recv):
    barrier = greet(nrows, ncols)
    row = lax.axis_index("row")
    col = lax.axis_index("col")
    num_slots = slot_rows.shape[1]
    lane = lax.broadcasted_iota(jnp.int32, (8, TILE), 1)
    sub = lax.broadcasted_iota(jnp.int32, (8, TILE), 0)
    own_row = pl.multiple_of(col * tiles, tiles)
    own_col = pl.multiple_of(row * tiles, tiles)

    for t in range(tiles):
        part = slice(t * TILE, (t + 1) * TILE)
        raw[t, 0:3, :] = pos[:, part]
        raw[t, 3:6, :] = strg[:, part]
        raw[t, 6:7, :] = cores[t : t + 1, :]
        raw[t, 7:8, :] = cores[t : t + 1, :]
    for t in range(tiles):
        spot = jnp.broadcast_to(order[t : t + 1, :], (8, TILE))
        inner = spot % TILE
        outer = spot // TILE
        found = jnp.zeros((8, TILE), jnp.float32)
        for s in range(tiles):
            found = jnp.where(outer == s, jnp.take_along_axis(raw[s], inner, axis=1), found)
        keep = (lane < counts[t]) | (sub < 3) | (sub > 5)
        found = jnp.where(keep, found, 0.0)
        row_blk[own_row + t] = found
        col_blk[own_col + t] = found

    pl.semaphore_wait(barrier, nrows + ncols - 2)
    copies = []
    for n, (axis, k) in enumerate(peers(nrows, ncols)):
        size, me, block, at = (ncols, col, row_blk, own_row) if axis == "col" else (nrows, row, col_blk, own_col)
        copy = pltpu.make_async_remote_copy(
            src_ref=block.at[pl.ds(at, tiles)],
            dst_ref=block.at[pl.ds(at, tiles)],
            send_sem=send.at[0, n],
            recv_sem=recv.at[0, n],
            device_id={axis: lax.rem(me + k, size)},
            device_id_type=MESH,
        )
        copy.start()
        copies.append(copy)

    stage[...] = jnp.zeros_like(stage)

    def weights(block, at, out):
        some = block.at[pl.ds(at, tiles)]
        x = [some[:, k, :] for k in range(3)]
        a = [some[:, 3 + k, :] for k in range(3)]
        for k, value in enumerate(a + cross(x, a)):
            high = value.astype(jnp.bfloat16).astype(jnp.float32)
            stage[:, k, :] = high
            stage[:, 6 + k, :] = value - high
        for t in range(tiles):
            both = stage[t].astype(jnp.bfloat16)
            out[at + t, :, 0:TILE] = both
            out[at + t, :, TILE:] = both

    def prepare_row(k):
        at = pl.multiple_of(lax.rem(col + k, ncols) * tiles, tiles)
        weights(row_blk, at, row_w)
        for t in range(tiles):
            across[at + t] = row_blk[at + t].T

    def prepare_col(k):
        weights(col_blk, pl.multiple_of(lax.rem(row + k, nrows) * tiles, tiles), col_w)

    def pair(u, s, ti, sj, react):
        src = col_blk[sj]
        xj = [src[k : k + 1, :] for k in range(7)]
        hj = 0.5 * xj[6] * xj[6]
        for c in range(TILE // CHUNK):
            at = slice(c * CHUNK, (c + 1) * CHUNK)
            at2 = slice(TILE + c * CHUNK, TILE + (c + 1) * CHUNK)
            tgt = across[ti, at, :]
            xi = [tgt[:, k : k + 1] for k in range(7)]
            hi = 0.5 * xi[6] * xi[6]
            dx = xi[0] - xj[0]
            dy = xi[1] - xj[1]
            dz = xi[2] - xj[2]
            s2 = hi + hj
            d = dx * dx + dy * dy + dz * dz + s2
            inv = lax.rsqrt(d)
            inv2 = inv * inv
            inv3 = inv2 * inv
            w = s2 * (inv3 * inv2)
            q = inv3 + 1.5 * w
            f = (q + w) * inv2
            g = f * (xi[3] * dx + xi[4] * dy + xi[5] * dz)
            q1, q2 = split(q)
            g1, g2 = split(g)
            tgt_buf[u, at, 0:TILE] = q1
            tgt_buf[u, at, TILE:] = q2
            tgt_buf[u, at2, 0:TILE] = g1
            tgt_buf[u, at2, TILE:] = g2
            if react:
                h = f * (xj[3] * dx + xj[4] * dy + xj[5] * dz)
                h1, h2 = split(h)
                src_buf[u, at, 0:TILE] = q1
                src_buf[u, at, TILE:] = h1
                src_buf[u, at2, 0:TILE] = q2
                src_buf[u, at2, TILE:] = h2
        out = lax.dot_general(col_w[sj], tgt_buf[u], (((1,), (1,)), ((), ())), preferred_element_type=jnp.float32)
        tgt_terms[s, 0:6, :] = out[0:6] + out[6:12]
        if react:
            out = lax.dot_general(row_w[ti], src_buf[u], (((1,), (0,)), ((), ())), preferred_element_type=jnp.float32)
            src_terms[s, 0:6, :] = out[0:6] + out[6:12]

    prepare_row(0)
    prepare_col(0)
    src_terms[0:tiles] = jnp.zeros((tiles, 8, 2 * TILE), jnp.float32)

    def diagonal(step, _):
        for u in range(2):
            t = step * 2 + u
            pair(u, t, own_row + t, own_col + t, False)
        return 0

    lax.fori_loop(0, tiles // 2, diagonal, 0)
    for copy in copies:
        copy.wait_recv()
    for k in range(1, ncols):
        prepare_row(k)
    for k in range(1, nrows):
        prepare_col(k)

    def visit(step, _):
        for u in range(UNROLL):
            s = tiles + step * UNROLL + u
            pair(u, s, slots[0, s], slots[1, s], True)
        return 0

    lax.fori_loop(0, (num_slots - tiles) // UNROLL, visit, 0)

    first = slot_rows[0:1, :]
    second = slot_rows[1:2, :]
    slot = lax.broadcasted_iota(jnp.int32, (1, num_slots), 1)
    first = jnp.where(slot < tiles, own_row + slot, first)
    gi = row * (ncols * tiles) + first
    gj = ((second // tiles) * ncols + col) * tiles + second % tiles
    alive = slot < count[0]
    row_sel = jnp.where(alive, first, -1)
    col_sel = jnp.where(alive & (gi != gj) & (slot >= tiles), second, -1)

    def finish(select, terms, block, out, sign):
        size = block.shape[0]
        here = lax.broadcasted_iota(jnp.int32, (size, num_slots), 0)
        hot = jnp.where(here == select, 1.0, 0.0).astype(jnp.bfloat16)
        qs, fs = [], []
        for k in range(6):
            high, low = split(terms[:, k, :])
            value = jnp.dot(hot, high, preferred_element_type=jnp.float32)
            value += jnp.dot(hot, low, preferred_element_type=jnp.float32)
            qs.append(value[:, 0:TILE])
            fs.append(value[:, TILE:])
        x = [block[:, k, :] for k in range(3)]
        a = [block[:, 3 + k, :] for k in range(3)]
        velocity = cross(x, qs[0:3])
        turn = cross(a, qs[0:3])
        steep = cross(x, fs[0:3])
        for k in range(3):
            v = biot_factor * (velocity[k] - qs[3 + k])
            w = biot_factor * (turn[k] - (3.0 * sign) * (steep[k] - fs[3 + k]))
            out[:, k] = v.reshape(size // tiles, tiles, TILE)
            out[:, 3 + k] = w.reshape(size // tiles, tiles, TILE)

    for copy in copies:
        copy.wait_send()

    def send_all(axis, first_sem, size, me, sums, held):
        started = []
        for k in range(1, size):
            other = lax.rem(me + k, size)
            copy = pltpu.make_async_remote_copy(
                src_ref=sums.at[other],
                dst_ref=held.at[k - 1],
                send_sem=send.at[1, first_sem + k - 1],
                recv_sem=recv.at[1, first_sem + k - 1],
                device_id={axis: other},
                device_id_type=MESH,
            )
            copy.start()
            started.append((copy, held.at[k - 1]))
        return started

    finish(row_sel, tgt_terms, row_blk, row_sum, 1.0)
    started = send_all("col", 0, ncols, col, row_sum, row_held)
    finish(col_sel, src_terms, col_blk, col_sum, -1.0)
    started += send_all("row", ncols - 1, nrows, row, col_sum, col_held)
    total = row_sum[col] + col_sum[row]
    for copy, held in started:
        copy.wait_recv()
        total = total + held[...]
    for t in range(tiles):
        part = slice(t * TILE, (t + 1) * TILE)
        live = lane[0:1, :] < counts[t]
        for k in range(3):
            vel[k : k + 1, part] = jnp.where(live, total[k, t : t + 1, :], 0.0)
            stretch[k : k + 1, part] = jnp.where(live, total[3 + k, t : t + 1, :], 0.0)
    for copy, _ in started:
        copy.wait_send()


def shards(nrows, ncols, positions, strengths, cores, order, tile_counts, pair_slots, pair_count):
    tiles = tile_counts.shape[0]
    num_slots = pair_slots.shape[1]
    others = nrows + ncols - 2
    nt, ns = ncols * tiles, nrows * tiles
    f32, bf16 = jnp.float32, jnp.bfloat16
    return pl.pallas_call(
        functools.partial(wake_kernel, nrows, ncols, tiles),
        out_shape=(
            jax.ShapeDtypeStruct((3, tiles * TILE), f32),
            jax.ShapeDtypeStruct((3, tiles * TILE), f32),
        ),
        in_specs=[SMEM, SMEM, SMEM, VMEM, VMEM, VMEM, VMEM, VMEM],
        out_specs=(VMEM, VMEM),
        scratch_shapes=[
            pltpu.VMEM((tiles, 8, TILE), f32),
            pltpu.VMEM((nt, 8, TILE), f32),
            pltpu.VMEM((ns, 8, TILE), f32),
            pltpu.VMEM((nt, TILE, 8), f32),
            pltpu.VMEM((tiles, 16, TILE), f32),
            pltpu.VMEM((nt, 16, 2 * TILE), bf16),
            pltpu.VMEM((ns, 16, 2 * TILE), bf16),
            pltpu.VMEM((UNROLL, 2 * TILE, 2 * TILE), bf16),
            pltpu.VMEM((UNROLL, 2 * TILE, 2 * TILE), bf16),
            pltpu.VMEM((num_slots, 8, 2 * TILE), f32),
            pltpu.VMEM((num_slots, 8, 2 * TILE), f32),
            pltpu.VMEM((ncols, 6, tiles, TILE), f32),
            pltpu.VMEM((nrows, 6, tiles, TILE), f32),
            pltpu.VMEM((ncols - 1, 6, tiles, TILE), f32),
            pltpu.VMEM((nrows - 1, 6, tiles, TILE), f32),
            pltpu.SemaphoreType.DMA((2, others)),
            pltpu.SemaphoreType.DMA((2, others)),
        ],
        compiler_params=pltpu.CompilerParams(
            collective_id=0, has_side_effects=True, vmem_limit_bytes=32 * 1024 * 1024
        ),
        name="wake",
    )(pair_slots, pair_count, tile_counts, pair_slots, positions, strengths,
      cores.reshape(tiles, TILE), order.reshape(tiles, TILE))


def solution(mesh):
    whole = ("groups", "row", "col")
    in_specs = (P(None, whole), P(None, whole), P(whole), P(whole), P(whole), P(None, whole), P(whole))
    out_specs = (P(None, whole), P(None, whole))
    body = functools.partial(shards, mesh.shape["row"], mesh.shape["col"])
    return jax.shard_map(body, mesh=mesh, in_specs=in_specs, out_specs=out_specs, check_vma=False)
```

time: 48.9 us -> 35.2 us (0.72); the launches traced: 49 us -> 34.7 us
  Pallas kernels: 42 us -> 29.4 us
  local copies, waits for them, and re-layouts: 5.72 us -> 3.99 us
    pallas_call x3 -> x1, Pallas kernels: 42 us -> 29.4 us  [shards(): pl.pallas_call(functools.partial(wake_kernel, nrows, ncols, tiles), out_s...]
    unnamed x14, local copies, waits for them, and re-layouts: 5.72 us -> 3.99 us
where the time goes in v2:
time: 35.2 us; the launch traced here: 34.7 us
  Pallas kernels  29.4 us (84%)
  local copies, waits for them, and re-layouts  3.99 us (11%)
  between operations  1.33 us (4%)
    pallas_call x1, Pallas kernels, shards(): pl.pallas_call(functools.partial(wake_kernel, nrows, ncols, tiles), out_s...  29.4 us
    unnamed x14, local copies, waits for them, and re-layouts  3.99 us

profile of v2, /device:TPU:0, one launch (start us, length us, event | category | flops | bytes accessed | tf_op | source)
XLA Modules:
  0.0 34.7 jit_solution(12624505414418252056)
XLA Ops:
  0.6 0.0 copy-start.3
  1.3 0.0 copy-start.2
  1.3 0.0 copy-start.5
  1.3 0.0 copy-done.3
  1.3 0.7 %copy-done.2 = s32[2,64]{1,0:T(2,128)S(1)} copy-done((s32[2,64]{1,0:T(2,128)S(1)}, s32[2,64]{1,0:T(2,128)}, u32[]{:S(2)}) %copy-start.2) | copy-done | bytes 536
  2.0 0.0 copy-done.5
  2.0 0.0 copy-start
  2.0 0.7 %copy-done = f32[3,1024]{1,0:T(4,128)S(1)} copy-done((f32[3,1024]{1,0:T(4,128)S(1)}, f32[3,1024]{1,0:T(4,128)}, u32[]{:S(2)}) %copy-start) | copy-done | bytes 12312
  2.7 0.0 copy-start.1
  2.7 0.7 %copy-done.1 = f32[3,1024]{1,0:T(4,128)S(1)} copy-done((f32[3,1024]{1,0:T(4,128)S(1)}, f32[3,1024]{1,0:T(4,128)}, u32[]{:S(2)}) %copy-start.1) | copy-done | bytes 12312
  3.4 0.0 copy-start.4
  3.4 0.7 %copy-done.4 = s32[1024]{0:T(1024)S(1)} copy-done((s32[1024]{0:T(1024)S(1)}, s32[1024]{0:T(1024)}, u32[]{:S(2)}) %copy-start.4) | copy-done | bytes 4120
  4.1 29.4 %wake.1 = (f32[3,1024]{1,0:T(4,128)S(1)}, f32[3,1024]{1,0:T(4,128)S(1)}) custom-call(s32[2,64]{1,0:T(2,128)S(1)} %copy-done.2, s32[1]{0:T(128)S(6)} %copy.11.count, s32[8]{0:T(128)S(1)} %copy-done.5, s32[2,64]{1,0:T(2,128)S(1)} %copy-done.2, f32[3,1024]{1,0:T(4,128)S(1)} %copy-done, f32[3,1024]{1,0:T(4,128)S(1)} %copy-done.1, f32[8,128]{1,0:T(8,128)S(1)} %bitcast.2, ...), custom_call_target="tpu_custom_call" | custom-call | tf_op jit(solution)/shard_map/wake/pallas_call | solution.py:254
  33.5 0.6 %copy.12 = f32[3,1024]{1,0:T(4,128)} copy(f32[3,1024]{1,0:T(4,128)S(1)} %get-tuple-element.4) | data formatting | bytes 24576
  34.1 0.6 %copy.13 = f32[3,1024]{1,0:T(4,128)} copy(f32[3,1024]{1,0:T(4,128)S(1)} %get-tuple-element.5) | data formatting | bytes 24576
Async XLA Ops:
  0.6 0.7 %copy-start.3 = (f32[1024]{0:T(1024)S(1)}, f32[1024]{0:T(1024)}, u32[]{:S(2)}) copy-start(f32[1024]{0:T(1024)} %param.9) | copy-start | bytes 12292
  1.3 0.7 %copy-start.2 = (s32[2,64]{1,0:T(2,128)S(1)}, s32[2,64]{1,0:T(2,128)}, u32[]{:S(2)}) copy-start(s32[2,64]{1,0:T(2,128)} %slot_rows.1) | copy-start | bytes 1540
  1.3 0.7 %copy-start.5 = (s32[8]{0:T(128)S(1)}, s32[8]{0:T(128)}, u32[]{:S(2)}) copy-start(s32[8]{0:T(128)} %counts.1) | copy-start | bytes 100
  2.0 0.7 %copy-start = (f32[3,1024]{1,0:T(4,128)S(1)}, f32[3,1024]{1,0:T(4,128)}, u32[]{:S(2)}) copy-start(f32[3,1024]{1,0:T(4,128)} %pos.1) | copy-start | bytes 36868
  2.7 0.7 %copy-start.1 = (f32[3,1024]{1,0:T(4,128)S(1)}, f32[3,1024]{1,0:T(4,128)}, u32[]{:S(2)}) copy-start(f32[3,1024]{1,0:T(4,128)} %strg.1) | copy-start | bytes 36868
  3.4 0.7 %copy-start.4 = (s32[1024]{0:T(1024)S(1)}, s32[1024]{0:T(1024)}, u32[]{:S(2)}) copy-start(s32[1024]{0:T(1024)} %param.10) | copy-start | bytes 12292

commit v3 on v2

--- a/solution.py
+++ b/solution.py
@@ -12,7 +12,8 @@
 MESH = pl.DeviceIdType.MESH
 VMEM = pl.BlockSpec(memory_space=pltpu.VMEM)
 SMEM = pl.BlockSpec(memory_space=pltpu.SMEM)
-UNROLL = 4
+HBM = pl.BlockSpec(memory_space=pltpu.HBM)
+UNROLL = 8
 CHUNK = 16
 
 biot_factor = -1.0 / (4.0 * math.pi)
@@ -40,9 +41,13 @@
     return [left[(k + 1) % 3] * right[(k + 2) % 3] - left[(k + 2) % 3] * right[(k + 1) % 3] for k in range(3)]
 
 
-def wake_kernel(nrows, ncols, tiles, slots, count, counts, slot_rows, pos, strg, cores, order,
-                vel, stretch, raw, row_blk, col_blk, across, stage, row_w, col_w, tgt_buf, src_buf,
-                tgt_terms, src_terms, row_sum, col_sum, row_held, col_held, send, recv):
+def wake_kernel(nrows, ncols, tiles, slots, count, counts, slot_rows_in, pos_in, strg_in, cores_in, order_in,
+                vel, stretch, slot_rows, pos, strg, cores, order, raw, row_blk, col_blk, spread, ones, stage, row_w, col_w, tgt_buf, src_buf,
+                tgt_terms, src_terms, row_sum, col_sum, row_held, col_held, load, send, recv):
+    pairs_in = [(pos_in, pos), (strg_in, strg), (cores_in, cores), (order_in, order), (slot_rows_in, slot_rows)]
+    loads = [pltpu.make_async_copy(src, dst, load.at[n]) for n, (src, dst) in enumerate(pairs_in)]
+    for copy in loads:
+        copy.start()
     barrier = greet(nrows, ncols)
     row = lax.axis_index("row")
     col = lax.axis_index("col")
@@ -52,6 +57,13 @@
     own_row = pl.multiple_of(col * tiles, tiles)
     own_col = pl.multiple_of(row * tiles, tiles)
 
+    stage[...] = jnp.zeros_like(stage)
+    rank = lax.broadcasted_iota(jnp.int32, (16, TILE), 0)
+    for k in range(3):
+        ones[:, k * TILE : (k + 1) * TILE] = jnp.where((rank == k) | (rank == 6 + k), 1.0, 0.0).astype(jnp.bfloat16)
+    ones[:, 3 * TILE :] = jnp.where((rank > 11) & (rank < 15), 1.0, 0.0).astype(jnp.bfloat16)
+    for copy in loads:
+        copy.wait()
     for t in range(tiles):
         part = slice(t * TILE, (t + 1) * TILE)
         raw[t, 0:3, :] = pos[:, part]
@@ -85,8 +97,6 @@
         copy.start()
         copies.append(copy)
 
-    stage[...] = jnp.zeros_like(stage)
-
     def weights(block, at, out):
         some = block.at[pl.ds(at, tiles)]
         x = [some[:, k, :] for k in range(3)]
@@ -95,6 +105,12 @@
             high = value.astype(jnp.bfloat16).astype(jnp.float32)
             stage[:, k, :] = high
             stage[:, 6 + k, :] = value - high
+        sigma = some[:, 6, :]
+        rest = 0.5 * sigma * sigma
+        for k in range(3):
+            high = rest.astype(jnp.bfloat16).astype(jnp.float32)
+            stage[:, 12 + k, :] = high
+            rest = rest - high
         for t in range(tiles):
             both = stage[t].astype(jnp.bfloat16)
             out[at + t, :, 0:TILE] = both
@@ -104,7 +120,13 @@
         at = pl.multiple_of(lax.rem(col + k, ncols) * tiles, tiles)
         weights(row_blk, at, row_w)
         for t in range(tiles):
-            across[at + t] = row_blk[at + t].T
+            column = row_blk[at + t].T
+            for j in range(3):
+                spread[at + t, j] = jnp.broadcast_to(column[:, j : j + 1], (TILE, TILE))
+            rest = lax.dot_general(row_w[at + t, :, 0:TILE], ones[...], (((0,), (0,)), ((), ())),
+                                   preferred_element_type=jnp.float32)
+            for j in range(4):
+                spread[at + t, 3 + j] = rest[:, j * TILE : (j + 1) * TILE]
 
     def prepare_col(k):
         weights(col_blk, pl.multiple_of(lax.rem(row + k, nrows) * tiles, tiles), col_w)
@@ -116,13 +138,11 @@
         for c in range(TILE // CHUNK):
             at = slice(c * CHUNK, (c + 1) * CHUNK)
             at2 = slice(TILE + c * CHUNK, TILE + (c + 1) * CHUNK)
-            tgt = across[ti, at, :]
-            xi = [tgt[:, k : k + 1] for k in range(7)]
-            hi = 0.5 * xi[6] * xi[6]
+            xi = [spread[ti, k, at, :] for k in range(7)]
             dx = xi[0] - xj[0]
             dy = xi[1] - xj[1]
             dz = xi[2] - xj[2]
-            s2 = hi + hj
+            s2 = xi[6] + hj
             d = dx * dx + dy * dy + dz * dz + s2
             inv = lax.rsqrt(d)
             inv2 = inv * inv
@@ -155,18 +175,16 @@
     src_terms[0:tiles] = jnp.zeros((tiles, 8, 2 * TILE), jnp.float32)
 
     def diagonal(step, _):
-        for u in range(2):
-            t = step * 2 + u
+        for u in range(4):
+            t = step * 4 + u
             pair(u, t, own_row + t, own_col + t, False)
         return 0
 
-    lax.fori_loop(0, tiles // 2, diagonal, 0)
+    lax.fori_loop(0, tiles // 4, diagonal, 0)
     for copy in copies:
         copy.wait_recv()
-    for k in range(1, ncols):
-        prepare_row(k)
-    for k in range(1, nrows):
-        prepare_col(k)
+    lax.fori_loop(1, ncols, lambda k, _: (prepare_row(k), 0)[1], 0)
+    lax.fori_loop(1, nrows, lambda k, _: (prepare_col(k), 0)[1], 0)
 
     def visit(step, _):
         for u in range(UNROLL):
@@ -257,13 +275,19 @@
             jax.ShapeDtypeStruct((3, tiles * TILE), f32),
             jax.ShapeDtypeStruct((3, tiles * TILE), f32),
         ),
-        in_specs=[SMEM, SMEM, SMEM, VMEM, VMEM, VMEM, VMEM, VMEM],
+        in_specs=[SMEM, SMEM, SMEM, HBM, HBM, HBM, HBM, HBM],
         out_specs=(VMEM, VMEM),
         scratch_shapes=[
+            pltpu.VMEM((2, num_slots), jnp.int32),
+            pltpu.VMEM((3, tiles * TILE), f32),
+            pltpu.VMEM((3, tiles * TILE), f32),
+            pltpu.VMEM((tiles, TILE), f32),
+            pltpu.VMEM((tiles, TILE), jnp.int32),
             pltpu.VMEM((tiles, 8, TILE), f32),
             pltpu.VMEM((nt, 8, TILE), f32),
             pltpu.VMEM((ns, 8, TILE), f32),
-            pltpu.VMEM((nt, TILE, 8), f32),
+            pltpu.VMEM((nt, 7, TILE, TILE), f32),
+            pltpu.VMEM((16, 4 * TILE), bf16),
             pltpu.VMEM((tiles, 16, TILE), f32),
             pltpu.VMEM((nt, 16, 2 * TILE), bf16),
             pltpu.VMEM((ns, 16, 2 * TILE), bf16),
@@ -275,11 +299,12 @@
             pltpu.VMEM((nrows, 6, tiles, TILE), f32),
             pltpu.VMEM((ncols - 1, 6, tiles, TILE), f32),
             pltpu.VMEM((nrows - 1, 6, tiles, TILE), f32),
+            pltpu.SemaphoreType.DMA((5,)),
             pltpu.SemaphoreType.DMA((2, others)),
             pltpu.SemaphoreType.DMA((2, others)),
         ],
         compiler_params=pltpu.CompilerParams(
-            collective_id=0, has_side_effects=True, vmem_limit_bytes=32 * 1024 * 1024
+            collective_id=0, has_side_effects=True, vmem_limit_bytes=56 * 1024 * 1024
         ),
         name="wake",
     )(pair_slots, pair_count, tile_counts, pair_slots, positions, strengths,

time: 35.2 us -> 28.8 us (0.82)
  Pallas kernels: 29.4 us -> 25.3 us
  local copies, waits for them, and re-layouts: 3.99 us -> 1.94 us
    pallas_call x1, Pallas kernels: 29.4 us -> 25.3 us  [shards(): pl.pallas_call(functools.partial(wake_kernel, nrows, ncols, tiles), out_s...]
    unnamed x14 -> x4, local copies, waits for them, and re-layouts: 3.99 us -> 1.94 us
where the time goes in v3:
time: 28.8 us; the launch traced here: 28.6 us
  Pallas kernels  25.3 us (88%)
  local copies, waits for them, and re-layouts  1.94 us (7%)
  between operations  1.3 us (5%)
    pallas_call x1, Pallas kernels, shards(): pl.pallas_call(functools.partial(wake_kernel, nrows, ncols, tiles), out_s...  25.3 us
    unnamed x4, local copies, waits for them, and re-layouts  1.94 us

profile of v3, /device:TPU:0, one launch (start us, length us, event | category | flops | bytes accessed | tf_op | source)
XLA Modules:
  0.0 28.6 jit_solution(12220295069692198044)
XLA Ops:
  1.3 25.3 %wake.1 = (f32[3,1024]{1,0:T(4,128)}, f32[3,1024]{1,0:T(4,128)}) custom-call(s32[2,64]{1,0:T(2,128)} %slot_rows_in.1, s32[1]{0:T(128)S(6)} %copy.11.count, s32[8]{0:T(128)} %counts.1, s32[2,64]{1,0:T(2,128)} %slot_rows_in.1, f32[3,1024]{1,0:T(4,128)} %pos_in.1, f32[3,1024]{1,0:T(4,128)} %strg_in.1, f32[8,128]{1,0:T(8,128)} %bitcast.2, s32[8,128]{1,0:T(8,128)} %bitcast.3), custom_call_target="tpu_custom_call" | custom-call | tf_op jit(solution)/shard_map/wake/pallas_call | solution.py:272
  26.6 0.0 copy-start
  26.6 1.3 %copy.12 = f32[3,1024]{1,0:T(4,128)} copy(f32[3,1024]{1,0:T(4,128)} %get-tuple-element.4) | data formatting | bytes 24576
  27.9 0.0 copy-done
  27.9 0.6 %copy.13 = f32[3,1024]{1,0:T(4,128)} copy(f32[3,1024]{1,0:T(4,128)S(1)} %copy-done) | data formatting | bytes 24576
Async XLA Ops:
  26.6 1.3 %copy-start = (f32[3,1024]{1,0:T(4,128)S(1)}, f32[3,1024]{1,0:T(4,128)}, u32[]{:S(2)}) copy-start(f32[3,1024]{1,0:T(4,128)} %get-tuple-element.5) | copy-start | bytes 36868

commit v4 on v3

--- a/solution.py
+++ b/solution.py
@@ -13,7 +13,7 @@
 VMEM = pl.BlockSpec(memory_space=pltpu.VMEM)
 SMEM = pl.BlockSpec(memory_space=pltpu.SMEM)
 HBM = pl.BlockSpec(memory_space=pltpu.HBM)
-UNROLL = 8
+UNROLL = 14
 CHUNK = 16
 
 biot_factor = -1.0 / (4.0 * math.pi)
@@ -42,7 +42,7 @@
 
 
 def wake_kernel(nrows, ncols, tiles, slots, count, counts, slot_rows_in, pos_in, strg_in, cores_in, order_in,
-                vel, stretch, slot_rows, pos, strg, cores, order, raw, row_blk, col_blk, spread, ones, stage, row_w, col_w, tgt_buf, src_buf,
+                sums_out, slot_rows, pos, strg, cores, order, raw, row_blk, col_blk, spread, ones, stage, row_w, col_w, tgt_buf, src_buf,
                 tgt_terms, src_terms, row_sum, col_sum, row_held, col_held, load, send, recv):
     pairs_in = [(pos_in, pos), (strg_in, strg), (cores_in, cores), (order_in, order), (slot_rows_in, slot_rows)]
     loads = [pltpu.make_async_copy(src, dst, load.at[n]) for n, (src, dst) in enumerate(pairs_in)]
@@ -72,8 +72,8 @@
         raw[t, 7:8, :] = cores[t : t + 1, :]
     for t in range(tiles):
         spot = jnp.broadcast_to(order[t : t + 1, :], (8, TILE))
-        inner = spot % TILE
-        outer = spot // TILE
+        inner = spot & (TILE - 1)
+        outer = spot >> 7
         found = jnp.zeros((8, TILE), jnp.float32)
         for s in range(tiles):
             found = jnp.where(outer == s, jnp.take_along_axis(raw[s], inner, axis=1), found)
@@ -117,7 +117,7 @@
             out[at + t, :, TILE:] = both
 
     def prepare_row(k):
-        at = pl.multiple_of(lax.rem(col + k, ncols) * tiles, tiles)
+        at = pl.multiple_of(lax.rem(col + ncols - k, ncols) * tiles, tiles)
         weights(row_blk, at, row_w)
         for t in range(tiles):
             column = row_blk[at + t].T
@@ -129,7 +129,7 @@
                 spread[at + t, 3 + j] = rest[:, j * TILE : (j + 1) * TILE]
 
     def prepare_col(k):
-        weights(col_blk, pl.multiple_of(lax.rem(row + k, nrows) * tiles, tiles), col_w)
+        weights(col_blk, pl.multiple_of(lax.rem(row + nrows - k, nrows) * tiles, tiles), col_w)
 
     def pair(u, s, ti, sj, react):
         src = col_blk[sj]
@@ -181,10 +181,26 @@
         return 0
 
     lax.fori_loop(0, tiles // 4, diagonal, 0)
-    for copy in copies:
-        copy.wait_recv()
-    lax.fori_loop(1, ncols, lambda k, _: (prepare_row(k), 0)[1], 0)
-    lax.fori_loop(1, nrows, lambda k, _: (prepare_col(k), 0)[1], 0)
+
+    def arrived(axis, size, me, block, base, prepare):
+        def step(k, _):
+            other = lax.rem(me + size - k, size)
+            place = block.at[pl.ds(pl.multiple_of(other * tiles, tiles), tiles)]
+            pltpu.make_async_remote_copy(
+                src_ref=place,
+                dst_ref=place,
+                send_sem=send.at[0, base + k - 1],
+                recv_sem=recv.at[0, base + k - 1],
+                device_id={axis: other},
+                device_id_type=MESH,
+            ).wait_recv()
+            prepare(k)
+            return 0
+
+        lax.fori_loop(1, size, step, 0)
+
+    arrived("col", ncols, col, row_blk, 0, prepare_row)
+    arrived("row", nrows, row, col_blk, ncols - 1, prepare_col)
 
     def visit(step, _):
         for u in range(UNROLL):
@@ -257,8 +273,8 @@
         part = slice(t * TILE, (t + 1) * TILE)
         live = lane[0:1, :] < counts[t]
         for k in range(3):
-            vel[k : k + 1, part] = jnp.where(live, total[k, t : t + 1, :], 0.0)
-            stretch[k : k + 1, part] = jnp.where(live, total[3 + k, t : t + 1, :], 0.0)
+            sums_out[k : k + 1, part] = jnp.where(live, total[k, t : t + 1, :], 0.0)
+            sums_out[3 + k : 4 + k, part] = jnp.where(live, total[3 + k, t : t + 1, :], 0.0)
     for copy, _ in started:
         copy.wait_send()
 
@@ -269,14 +285,11 @@
     others = nrows + ncols - 2
     nt, ns = ncols * tiles, nrows * tiles
     f32, bf16 = jnp.float32, jnp.bfloat16
-    return pl.pallas_call(
+    sums = pl.pallas_call(
         functools.partial(wake_kernel, nrows, ncols, tiles),
-        out_shape=(
-            jax.ShapeDtypeStruct((3, tiles * TILE), f32),
-            jax.ShapeDtypeStruct((3, tiles * TILE), f32),
-        ),
+        out_shape=jax.ShapeDtypeStruct((6, tiles * TILE), f32),
         in_specs=[SMEM, SMEM, SMEM, HBM, HBM, HBM, HBM, HBM],
-        out_specs=(VMEM, VMEM),
+        out_specs=VMEM,
         scratch_shapes=[
             pltpu.VMEM((2, num_slots), jnp.int32),
             pltpu.VMEM((3, tiles * TILE), f32),
@@ -309,6 +322,7 @@
         name="wake",
     )(pair_slots, pair_count, tile_counts, pair_slots, positions, strengths,
       cores.reshape(tiles, TILE), order.reshape(tiles, TILE))
+    return sums[0:3], sums[3:6]
 
 
 def solution(mesh):

time: 28.8 us -> 27.3 us (0.948)
  Pallas kernels: 25.3 us -> 24.3 us
  local copies, waits for them, and re-layouts: 1.94 us -> 1.45 us
    unnamed x4 -> x0, local copies, waits for them, and re-layouts: 1.94 us -> none
    slice x0 -> x1, local copies, waits for them, and re-layouts: none -> 1.45 us  [shards(): return (sums[0:3], sums[3:6])]
    pallas_call x1, Pallas kernels: 25.3 us -> 24.3 us  [shards(): pl.pallas_call(functools.partial(wake_kernel, nrows, ncols, tiles), out_s...]
where the time goes in v4:
time: 27.3 us; the launch traced here: 27 us
  Pallas kernels  24.3 us (89%)
  local copies, waits for them, and re-layouts  1.45 us (5%)
  between operations  1.29 us (5%)
    pallas_call x1, Pallas kernels, shards(): pl.pallas_call(functools.partial(wake_kernel, nrows, ncols, tiles), out_s...  24.3 us
    slice x1, local copies, waits for them, and re-layouts, shards(): return (sums[0:3], sums[3:6])  1.45 us

profile of v4, /device:TPU:0, one launch (start us, length us, event | category | flops | bytes accessed | tf_op | source)
XLA Modules:
  0.0 27.0 jit_solution(5332338676541300161)
XLA Ops:
  1.3 24.3 %wake.1 = f32[6,1024]{1,0:T(8,128)} custom-call(s32[2,64]{1,0:T(2,128)} %slot_rows_in.1, s32[1]{0:T(128)S(6)} %copy.9.count, s32[8]{0:T(128)} %counts.1, s32[2,64]{1,0:T(2,128)} %slot_rows_in.1, f32[3,1024]{1,0:T(4,128)} %pos_in.1, f32[3,1024]{1,0:T(4,128)} %strg_in.1, f32[8,128]{1,0:T(8,128)} %bitcast.2, s32[8,128]{1,0:T(8,128)} %bitcast.3), custom_call_target="tpu_custom_call" | custom-call | tf_op jit(solution)/shard_map/wake/pallas_call | solution.py:288
  25.6 1.5 %fusion = (f32[3,1024]{1,0:T(4,128)}, f32[3,1024]{1,0:T(4,128)}) fusion(f32[6,1024]{1,0:T(8,128)} %wake.1), kind=kLoop, calls=%fused_computation | loop fusion | bytes 49152 | tf_op jit(solution)/shard_map/slice | solution.py:325
